TPU v7x, 32 devices: a whole 2x2x4 slice. The times are simulated.
32 devices in a mesh: groups: 2 (over x), tok: 16 (over z, y, core).
Axes of the slice: x: 2, y: 2, z: 4, core: 2. Of those that a mesh axis runs over, the one named last changes fastest.
Arguments:
- vis_query: bfloat16 [8192, 1280], P(('groups', 'tok')), parts along dimension 0, may hold values from -180 to 180
- vis_keyvalue: bfloat16 [2, 8192, 1280], P(None, ('groups', 'tok')), parts along dimension 1, may hold values from -6 to 6
- vis_residual: bfloat16 [8192, 1280], P(('groups', 'tok')), parts along dimension 0, may hold values from -4 to 4
- vis_out_weight: bfloat16 [1280, 1280], P('tok'), may hold values from -0.15625 to 0.15625
- vis_out_bias: float32 [1280], replicated, may hold values from -4 to 4
- image_units: int32 [96], P('groups'), parts along dimension 0, may hold values from 1 to 32, 1024 in all
- text_embed: bfloat16 [8192, 5120], P(('groups', 'tok')), parts along dimension 0, may hold values from -6 to 6
- lm_gain: float32 [5120], replicated, may hold values from 0.1 to 1.9
- lm_kv_weight: bfloat16 [5120, 2048], P(None, 'tok'), may hold values from -0.078125 to 0.078125
- lm_kv_bias: float32 [2048], replicated, may hold values from -6 to 6
- text_positions: int32 [8192], P(('groups', 'tok')), parts along dimension 0, may hold values from 0 to 4095
- image_destination: int32 [2048, 1], P(('groups', 'tok')), parts along dimension 0, may hold values from 0 to 15; in each aligned block of 64 rows (0 to 63, 64 to 127, ...) at most 8 rows name the same one
- image_positions: int32 [3, 4096], P(None, ('groups', 'tok')), parts along dimension 1, may hold values from 0 to 4095
Outputs:
- text_cache: bfloat16 [8192, 2048], P(('groups', 'tok')), parts along dimension 0
- image_cache: bfloat16 [4096, 2048], P(('groups', 'tok')), parts along dimension 0
There are 2 independent parts, one for each index of `groups`. A program takes and returns all parts, laid end to end along the dimension named above; an argument that names none is the same for every part. Nothing has to cross between parts.
Inputs may be any that keep to these rules, and one draw needn't show every extreme that they name: `image_units`: each image spans whole merged rows; entries sum to 1024 and one reaches the largest value. `image_destination`: among the 64 rows of one device no destination appears more than 8 times, and some device's rows reach that count.
All inputs are finite; a program needn't handle non-finite values.
Results may differ from a plain program's by a relative error of at most 0.0052.
Values may be sent and summed in bfloat16 or wider, within the bound.
A program may use at most 128 MiB of HBM per device.

v0:
```python
import math

import jax
import jax.numpy as jnp
from jax import lax
from jax.sharding import PartitionSpec as P

VIS_HEADS = 16
KV_HEADS = 8
LM_HEAD = 128


norm_epsilon = 1e-06
rope_base = 1000000.0


def with_halo(block, sides, width):
    for axis, dim in sides:
        count = lax.axis_size(axis)
        forward = [(i, i + 1) for i in range(count - 1)]
        backward = [(target, source) for source, target in forward]
        low = lax.ppermute(
            lax.slice_in_dim(block, block.shape[dim] - width, None, axis=dim), axis, forward
        )
        high = lax.ppermute(lax.slice_in_dim(block, 0, width, axis=dim), axis, backward)
        block = jnp.concatenate([low, block, high], axis=dim)
    return block


def segment_ids(global_index, bounds):
    return jnp.sum((global_index[:, None] >= bounds[None, :]).astype(jnp.int32), axis=1) - 1


def rms_scale(rows, gain):
    values = rows.astype(jnp.float32)
    mean_square = jnp.mean(values * values, axis=1, keepdims=True)
    return (values * lax.rsqrt(mean_square + norm_epsilon) * gain).astype(jnp.bfloat16)


def rotate_keys(values, bias, positions):
    shifted = values + bias
    row_count = shifted.shape[0]
    kv_half = shifted.shape[1] // 2
    half_size = LM_HEAD // 2
    key_part = shifted[:, :kv_half].reshape(row_count, KV_HEADS, LM_HEAD)
    lower_half = key_part[:, :, :half_size]
    upper_half = key_part[:, :, half_size:]
    index_pair = jnp.arange(half_size, dtype=jnp.int32)
    frequency = jnp.power(jnp.float32(rope_base), -2.0 * index_pair.astype(jnp.float32) / LM_HEAD)
    section = (index_pair >= half_size // 4).astype(jnp.int32) + (
        index_pair >= half_size // 4 + 3 * half_size // 8
    ).astype(jnp.int32)
    places = positions.astype(jnp.float32)
    chosen = jnp.zeros((row_count, half_size), jnp.float32)
    for axis_number in range(3):
        chosen = (
            chosen
            + places[axis_number][:, None] * (section == axis_number).astype(jnp.float32)[None, :]
        )
    angles = chosen * frequency[None, :]
    cosine = jnp.cos(angles)[:, None, :]
    sine_part = jnp.sin(angles)[:, None, :]
    turned = jnp.concatenate(
        [
            lower_half * cosine - upper_half * sine_part,
            upper_half * cosine + lower_half * sine_part,
        ],
        axis=2,
    )
    return jnp.concatenate(
        [turned.reshape(row_count, kv_half), shifted[:, kv_half:]], axis=1
    ).astype(jnp.bfloat16)


def head_attention(query_head, key_head, value_head, allowed, score_scale):
    scores = (
        jnp.einsum("qd,kd->qk", query_head, key_head, preferred_element_type=jnp.float32)
        * score_scale
    )
    scores = jnp.where(allowed, scores, -1e30)
    row_max = jnp.max(scores, axis=1, keepdims=True)
    shifted = jnp.exp(scores - row_max)
    weights = (shifted / jnp.sum(shifted, axis=1, keepdims=True)).astype(jnp.bfloat16)
    return jnp.dot(weights, value_head, preferred_element_type=jnp.float32).astype(jnp.bfloat16)


def project_rows(normed, kv_weight):
    return jnp.dot(
        normed,
        lax.all_gather(kv_weight, "tok", axis=1, tiled=True),
        preferred_element_type=jnp.float32,
    )


def per_device(
    vis_query,
    vis_keyvalue,
    vis_residual,
    vis_out_weight,
    vis_out_bias,
    image_units,
    text_embed,
    lm_gain,
    lm_kv_weight,
    lm_kv_bias,
    text_positions,
    image_destination,
    image_positions,
):
    patch_count, vis_width = vis_query.shape
    head_size = vis_width // VIS_HEADS
    half_window = patch_count // 2
    device_count = lax.axis_size("tok")
    device_index = lax.axis_index("tok")
    nearby = with_halo(vis_keyvalue, (("tok", 1),), half_window)
    bounds = jnp.concatenate([jnp.zeros((1,), jnp.int32), jnp.cumsum(4 * image_units)])
    offset = device_index * patch_count
    query_ids = segment_ids(offset + jnp.arange(patch_count, dtype=jnp.int32), bounds)
    key_ids = segment_ids(
        offset - half_window + jnp.arange(2 * patch_count, dtype=jnp.int32), bounds
    )
    allowed = query_ids[:, None] == key_ids[None, :]
    score_scale = 1.0 / math.sqrt(head_size)
    query_heads = vis_query.reshape(patch_count, VIS_HEADS, head_size).transpose(1, 0, 2)
    key_heads = nearby[0].reshape(2 * patch_count, VIS_HEADS, head_size).transpose(1, 0, 2)
    value_heads = nearby[1].reshape(2 * patch_count, VIS_HEADS, head_size).transpose(1, 0, 2)
    attended = lax.map(
        lambda pieces: head_attention(pieces[0], pieces[1], pieces[2], allowed, score_scale),
        (query_heads, key_heads, value_heads),
    )
    attended = attended.transpose(1, 0, 2).reshape(patch_count, vis_width)
    projected = jnp.dot(
        attended,
        lax.all_gather(vis_out_weight, "tok", axis=0, tiled=True),
        preferred_element_type=jnp.float32,
    )
    vis_hidden = (projected + vis_out_bias + vis_residual.astype(jnp.float32)).astype(jnp.bfloat16)
    merged = vis_hidden.reshape(patch_count // 4, 4 * vis_width)
    target = image_destination[:, 0]
    unit_count = target.shape[0]
    same_target = target[:, None] == target[None, :]
    earlier = (
        jnp.arange(unit_count, dtype=jnp.int32)[None, :]
        < jnp.arange(unit_count, dtype=jnp.int32)[:, None]
    )
    slot_rank = jnp.sum((same_target & earlier).astype(jnp.int32), axis=1)
    slot_count = image_positions.shape[1]
    capacity = slot_count // device_count
    slot_index = target * capacity + slot_rank
    text_count = text_embed.shape[0]
    kv_width = lm_kv_bias.shape[0]
    normed = rms_scale(jnp.concatenate([text_embed, merged], axis=0), lm_gain)
    projected_rows = project_rows(normed, lm_kv_weight)
    text_values = projected_rows[:text_count]
    outgoing = (
        jnp.zeros((slot_count, kv_width), jnp.float32)
        .at[slot_index]
        .set(projected_rows[text_count:])
    )
    image_values = lax.all_to_all(outgoing, "tok", split_axis=0, concat_axis=0, tiled=True)
    text_cache = rotate_keys(
        text_values, lm_kv_bias, jnp.broadcast_to(text_positions[None, :], (3, text_count))
    )
    image_cache = rotate_keys(image_values, lm_kv_bias, image_positions)
    return (text_cache, image_cache)


def solution(mesh):
    placed = (
        P(("groups", "tok"), None),
        P(None, ("groups", "tok"), None),
        P(("groups", "tok"), None),
        P("tok", None),
        P(),
        P("groups"),
        P(("groups", "tok"), None),
        P(),
        P(None, "tok"),
        P(),
        P(("groups", "tok")),
        P(("groups", "tok"), None),
        P(None, ("groups", "tok")),
    )
    return jax.shard_map(
        per_device,
        mesh=mesh,
        in_specs=placed,
        out_specs=(P(("groups", "tok"), None), P(("groups", "tok"), None)),
        check_vma=False,
    )
```

profile of v0, /device:TPU:9, one launch (start us, length us, event | category | flops | bytes accessed | tf_op | source)
XLA Modules:
  0.0 231.8 jit_solution(16934681712215817094)
XLA Ops:
  8.7 1.6 copy.33
  10.3 1.2 fusion.38
  11.4 3.7 %collective-permute-start = (bf16[2,128,1280]{1,2,0:T(8,128)(2,1)}, bf16[2,128,1280]{1,2,0:T(8,128)(2,1)S(1)}, u32[]{:S(2)}, u32[]{:S(2)}) collective-permute-start(bf16[2,128,1280]{1,2,0:T(8,128)(2,1)} %get-tuple-element.94), channel_id=1, source_target_pairs={{0,1},{1,2},{2,3},{3,4},{4,5},{5,6},{6,7},{7,8},{8,9},{9,10},{10,1... | collective-permute-start | bytes 1966088 | tf_op jit(solution)/shard_map/ppermute | solution.py:22
  15.1 1.9 collective-permute-start.1
  17.4 2.2 copy.32
  20.1 11.6 %collective-permute-done = bf16[2,128,1280]{1,2,0:T(8,128)(2,1)S(1)} collective-permute-done((bf16[2,128,1280]{1,2,0:T(8,128)(2,1)}, bf16[2,128,1280]{1,2,0:T(8,128)(2,1)S(1)}, u32[]{:S(2)}, u32[]{:S(2)}) %collective-permute-start) | collective-permute-done | bytes 655392 | tf_op jit(solution)/shard_map/ppermute | solution.py:22
  31.7 2.3 %collective-permute-done.1 = bf16[2,128,1280]{1,2,0:T(8,128)(2,1)S(1)} collective-permute-done((bf16[2,128,1280]{1,2,0:T(8,128)(2,1)S(1)}, bf16[2,128,1280]{1,2,0:T(8,128)(2,1)S(1)}, u32[]{:S(2)}, u32[]{:S(2)}) %collective-permute-start.1) | collective-permute-done | bytes 655392 | tf_op jit(solution)/shard_map/ppermute | solution.py:25
  34.6 36.6 %while.11 = (s32[]{:T(128)}, bf16[16,256,80]{1,2,0:T(8,128)(2,1)}, bf16[16,256,80]{1,2,0:T(8,128)(2,1)}, bf16[16,512,80]{1,2,0:T(8,128)(2,1)S(1)}, bf16[16,512,8...) while((s32[]{:T(128)}, bf16[16,256,80]{1,2,0:T(8,128)(2,1)}, ...), condition=%wide.region_6.7_spmd.clone, body=%wide.region_3.6_spmd.clone.sunk | while | flops 43142656 | bytes 1828949 | solution.py:127
  34.6 1.2 fusion.47
  36.9 1.1 fusion.47
  39.2 1.1 fusion.47
  41.5 1.1 fusion.47
  43.8 1.1 fusion.47
  46.1 1.1 fusion.47
  48.3 1.1 fusion.47
  50.6 1.1 fusion.47
  52.9 1.1 fusion.47
  55.2 1.1 fusion.47
  57.5 1.1 fusion.47
  59.8 1.1 fusion.47
  62.0 1.1 fusion.47
  64.3 1.1 fusion.47
  66.6 1.1 fusion.47
  68.9 1.1 fusion.47
  71.2 4.3 %fusion.24 = bf16[256,1280]{1,0:T(8,128)(2,1)} fusion(bf16[256,1280]{0,1:T(8,128)(2,1)} %bitcast.85, bf16[1280,1280]{1,0:T(8,128)(2,1)} %all-gather.3.cloned.1.call-done, bf16[256,1280]{1,0:T(8,128)(2,1)S(1)} %copy-done.4, f32[1280]{0:T(1024)S(1)} %copy-done.6), kind=kOutput, calls=%fused_computation.32 | convolution fusion | flops 840171520 | bytes 5248000 | tf_op jit(solution)/shard_map/dot_general | solution.py:132
  75.5 1.5 reshape.451
  77.8 101.0 %all-gather.5.cloned.1.call-done = bf16[5120,2048]{1,0:T(8,128)(2,1)} async-done(((bf16[5120,128]{1,0:T(8,128)(2,1)}), bf16[5120,2048]{1,0:T(8,128)(2,1)}) %all-gather.5.cloned.1.call-update) | async-done | bytes 20971536 | tf_op jit(solution)/shard_map/all_gather | solution.py:90
  178.8 12.4 %fusion.19 = f32[320,2048]{1,0:T(8,128)} fusion(bf16[5120,2048]{1,0:T(8,128)(2,1)} %all-gather.5.cloned.1.call-done, f32[5120]{0:T(1024)S(1)} %copy-done.5, f32[320]{0:T(512)S(1)} %add_rsqrt_fusion, bf16[64,5120]{1,0:T(8,128)(2,1)S(1)} %reshape.451, bf16[256,5120]{1,0:T(8,128)(2,1)S(1)} %copy-done), kind=kOutput, calls=%fused_computation.25 | convolution fusion | flops 6722355200 | bytes 26891520 | tf_op jit(solution)/shard_map/dot_general | solution.py:88
  191.2 2.4 %scatter_custom_fusion = f32[128,2048]{1,0:T(8,128)} fusion(s32[64]{0:T(128)S(1)} %fusion.34, f32[320,2048]{1,0:T(8,128)} %fusion.19, f32[]{:T(128)} %constant.27.clone.1), kind=kCustom, calls=%fused_computation.43 | custom fusion | bytes 1573376 | tf_op jit(solution)/shard_map/scatter | solution.py:158
  193.6 4.8 %all-to-all-start = ((f32[16,8,2048]{2,1,0:T(8,128)}), f32[16,8,2048]{2,1,0:T(8,128)S(1)}, u32[]{:S(2)}, u32[]{:S(2)}) async-start(f32[16,8,2048]{2,1,0:T(8,128)} %bitcast.12), calls=%async_computation | async-start | bytes 2097152 | tf_op jit(solution)/shard_map/all_to_all | solution.py:160
  199.5 1.8 slice_add_fusion
  203.6 19.7 %all-to-all-done = f32[16,8,2048]{2,1,0:T(8,128)S(1)} async-done(((f32[16,8,2048]{2,1,0:T(8,128)}), f32[16,8,2048]{2,1,0:T(8,128)S(1)}, u32[]{:S(2)}, u32[]{:S(2)}) %all-to-all-start) | async-done | bytes 1048608 | tf_op jit(solution)/shard_map/all_to_all | solution.py:160
  (98 shorter events, 26.9 us)
Async XLA Ops:
  7.2 64.0 %all-gather.3.cloned.1.call-start = ((), (), s32[]{:S(2)}) async-start(), calls=%async_computation.1 | async-start | bytes 3481600 | tf_op jit(solution)/shard_map/all_gather | solution.py:134
  7.9 170.9 %all-gather.5.cloned.1.call-start = ((), (), s32[]{:S(2)}) async-start(), calls=%async_computation.2 | async-start | bytes 22282240 | tf_op jit(solution)/shard_map/all_gather | solution.py:90
  8.6 8.4 %copy-start.7 = (s32[48]{0:T(128)S(1)}, s32[48]{0:T(128)}, u32[]{:S(2)}) copy-start(s32[48]{0:T(128)} %param.20) | copy-start | bytes 580
  10.3 9.3 %copy-start.2 = (s32[3,128]{1,0:T(4,128)S(1)}, s32[3,128]{1,0:T(4,128)}, u32[]{:S(2)}) copy-start(s32[3,128]{1,0:T(4,128)} %param.27) | copy-start | bytes 4612
  10.3 9.4 %copy-start.8 = (s32[64,1]{0,1:T(1,128)S(1)}, s32[64,1]{0,1:T(1,128)}, u32[]{:S(2)}) copy-start(s32[64,1]{0,1:T(1,128)} %param.26) | copy-start | bytes 772
  11.4 20.3 %collective-permute-start = (bf16[2,128,1280]{1,2,0:T(8,128)(2,1)}, bf16[2,128,1280]{1,2,0:T(8,128)(2,1)S(1)}, u32[]{:S(2)}, u32[]{:S(2)}) collective-permute-start(bf16[2,128,1280]{1,2,0:T(8,128)(2,1)} %get-tuple-element.94), channel_id=1, source_target_pairs={{0,1},{1,2},{2,3},{3,4},{4,5},{5,6},{6,7},{7,8},{8,9},{9,10},{10,1... | collective-permute-start | bytes 1966088 | tf_op jit(solution)/shard_map/ppermute | solution.py:22
  15.1 18.9 %collective-permute-start.1 = (bf16[2,128,1280]{1,2,0:T(8,128)(2,1)S(1)}, bf16[2,128,1280]{1,2,0:T(8,128)(2,1)S(1)}, u32[]{:S(2)}, u32[]{:S(2)}) collective-permute-start(bf16[2,128,1280]{1,2,0:T(8,128)(2,1)S(1)} %get-tuple-element.95), channel_id=1, source_target_pairs={{1,0},{2,1},{3,2},{4,3},{5,4},{6,5},{7,6},{8,7},{9,8},{10,9},{11,1... | collective-permute-start | bytes 1966088 | tf_op jit(solution)/shard_map/ppermute | solution.py:25
  34.5 36.6 %copy-start.4 = (bf16[256,1280]{1,0:T(8,128)(2,1)S(1)}, bf16[256,1280]{1,0:T(8,128)(2,1)}, u32[]{:S(2)}) copy-start(bf16[256,1280]{1,0:T(8,128)(2,1)} %param.17) | copy-start | bytes 1966084
  34.6 36.6 %copy-start.6 = (f32[1280]{0:T(1024)S(1)}, f32[1280]{0:T(1024)}, u32[]{:S(2)}) copy-start(f32[1280]{0:T(1024)} %param.19) | copy-start | bytes 15364
  71.2 5.8 %copy-start = (bf16[256,5120]{1,0:T(8,128)(2,1)S(1)}, bf16[256,5120]{1,0:T(8,128)(2,1)}, u32[]{:S(2)}) copy-start(bf16[256,5120]{1,0:T(8,128)(2,1)} %param.21) | copy-start | bytes 7864324
  75.5 103.3 %copy-start.5 = (f32[5120]{0:T(1024)S(1)}, f32[5120]{0:T(1024)}, u32[]{:S(2)}) copy-start(f32[5120]{0:T(1024)} %param.22) | copy-start | bytes 61444
  191.2 7.7 %copy-start.3 = (s32[256]{0:T(256)S(1)}, s32[256]{0:T(256)}, u32[]{:S(2)}) copy-start(s32[256]{0:T(256)} %param.25) | copy-start | bytes 3076
  191.2 8.2 %copy-start.1 = (f32[2048]{0:T(1024)S(1)}, f32[2048]{0:T(1024)}, u32[]{:S(2)}) copy-start(f32[2048]{0:T(1024)} %param.24) | copy-start | bytes 24580
  193.6 29.7 %all-to-all-start = ((f32[16,8,2048]{2,1,0:T(8,128)}), f32[16,8,2048]{2,1,0:T(8,128)S(1)}, u32[]{:S(2)}, u32[]{:S(2)}) async-start(f32[16,8,2048]{2,1,0:T(8,128)} %bitcast.12), calls=%async_computation | async-start | bytes 2097152 | tf_op jit(solution)/shard_map/all_to_all | solution.py:160
Sparse Core Ops, SparseCore 0:
  10.3 52.5 all-gather.2
  64.4 114.3 all-gather.4
where the time goes:
time: 233 us; the launch traced here: 232 us
  waiting for transfers between devices  136 us (58%)
  matrix products  49.6 us (21%)
  between operations  14.4 us (6%)
  other arithmetic  11.2 us (5%)
  starting transfers between devices  10.5 us (5%)
  local copies, waits for them, and re-layouts  10.1 us (4%)
    all_gather x1, waiting for transfers between devices, project_rows(): lax.all_gather(kv_weight, 'tok', axis=1, tiled=True)  101 us
    all_to_all x1, waiting for transfers between devices, per_device(): lax.all_to_all(outgoing, 'tok', split_axis=0, concat_axis=0, tiled=True)  19.7 us
    dot_general x16, matrix products, head_attention(): jnp.einsum('qd,kd->qk', query_head, key_head, preferred_element_type=jnp....  17.9 us
    dot_general x16, matrix products, head_attention(): jnp.dot(weights, value_head, preferred_element_type=jnp.float32)  15 us
    dot_general x1, matrix products, project_rows(): jnp.dot(normed, lax.all_gather(kv_weight, 'tok', axis=1, tiled=True), pre...  12.4 us
    ppermute x1, waiting for transfers between devices, with_halo(): lax.ppermute(lax.slice_in_dim(block, block.shape[dim] - width, None, axis...  11.6 us
    all_to_all x1, starting transfers between devices, per_device(): lax.all_to_all(outgoing, 'tok', split_axis=0, concat_axis=0, tiled=True)  4.8 us
  transfers between devices with their start and end apart: 5, of which 4 were waited for; matrix products, arithmetic and copies ran while one was open for 23% of the time, Pallas kernels for 0%

commit v1 on v0

--- a/solution.py
+++ b/solution.py
@@ -1,8 +1,11 @@
+import functools
 import math
 
 import jax
 import jax.numpy as jnp
 from jax import lax
+from jax.experimental import pallas as pl
+from jax.experimental.pallas import tpu as pltpu
 from jax.sharding import PartitionSpec as P
 
 VIS_HEADS = 16
@@ -25,6 +28,11 @@
         high = lax.ppermute(lax.slice_in_dim(block, 0, width, axis=dim), axis, backward)
         block = jnp.concatenate([low, block, high], axis=dim)
     return block
+
+
+def running_sums(counts):
+    index = jnp.arange(counts.shape[0], dtype=jnp.int32)
+    return jnp.sum(jnp.where(index[None, :] <= index[:, None], counts[None, :], 0), axis=1)
 
 
 def segment_ids(global_index, bounds):
@@ -113,7 +121,7 @@
     device_count = lax.axis_size("tok")
     device_index = lax.axis_index("tok")
     nearby = with_halo(vis_keyvalue, (("tok", 1),), half_window)
-    bounds = jnp.concatenate([jnp.zeros((1,), jnp.int32), jnp.cumsum(4 * image_units)])
+    bounds = jnp.concatenate([jnp.zeros((1,), jnp.int32), running_sums(4 * image_units)])
     offset = device_index * patch_count
     query_ids = segment_ids(offset + jnp.arange(patch_count, dtype=jnp.int32), bounds)
     key_ids = segment_ids(
@@ -163,6 +171,517 @@
     )
     image_cache = rotate_keys(image_values, lm_kv_bias, image_positions)
     return (text_cache, image_cache)
+
+
+MESH = pl.DeviceIdType.MESH
+
+
+def fused_kernel(
+    dims,
+    query_ref,
+    keyvalue_ref,
+    residual_ref,
+    out_bias_ref,
+    query_id_ref,
+    key_id_ref,
+    place_ref,
+    gain_ref,
+    bias_ref,
+    cosine_ref,
+    sine_ref,
+    text_ref,
+    out_shard_ref,
+    kv_shard_ref,
+    text_cache_ref,
+    image_cache_ref,
+    out_weight,
+    kv_weight,
+    nearby,
+    attended,
+    text_rows,
+    rows,
+    outgoing,
+    incoming,
+    total,
+    sib_send,
+    x_send,
+    y_send,
+    z_send,
+    recv,
+    halo_send,
+    halo_recv,
+    row_send,
+    row_recv,
+    local,
+):
+    count, depth = dims
+    group = lax.axis_index("groups")
+    me = lax.axis_index("tok")
+    core = lax.rem(me, 2)
+    chip = me // 2
+    y = lax.rem(chip, 2)
+    z = chip // 2
+    x = group
+    sibling = (group, me + 1 - 2 * core)
+    x_peer = (1 - group, me)
+    y_peer = (group, me + 2 - 4 * y)
+    right = lax.rem(me + 1, count)
+    left = lax.rem(me + count - 1, count)
+    patches, vis_width = query_ref.shape
+    window = patches // 2
+    text_count, width = text_ref.shape
+    slots = image_cache_ref.shape[0]
+
+    def along(step):
+        return lax.rem(z + step, depth)
+
+    def shard_of(level, row, lane):
+        return (level * 2 + row) * 2 + lane
+
+    copies = [
+        pltpu.make_async_copy(out_shard_ref, out_weight.at[me], local.at[0]),
+        pltpu.make_async_copy(kv_shard_ref, kv_weight.at[me], local.at[1]),
+        pltpu.make_async_copy(
+            keyvalue_ref, nearby.at[:, pl.ds(window, patches), :], local.at[2]
+        ),
+        pltpu.make_async_copy(text_ref, text_rows, local.at[3]),
+    ]
+    for copy in copies:
+        copy.start()
+
+    barrier = pltpu.get_barrier_semaphore()
+    for step in range(1, count):
+        pl.semaphore_signal(
+            barrier,
+            inc=1,
+            device_id=(group, lax.rem(me + step, count)),
+            device_id_type=MESH,
+        )
+    pl.semaphore_signal(barrier, inc=1, device_id=x_peer, device_id_type=MESH)
+    pl.semaphore_wait(barrier, count)
+
+    halves = (out_weight.shape[2] // 2, kv_weight.shape[1] // 2)
+
+    def chunk(kind, shard, half):
+        size = halves[kind]
+        if kind == 0:
+            return out_weight.at[shard, :, pl.ds(pl.multiple_of(half * size, 128), size)]
+        return kv_weight.at[shard, pl.ds(pl.multiple_of(half * size, 16), size), :]
+
+    def remote(kind, shard, half, sem, target):
+        return pltpu.make_async_remote_copy(
+            src_ref=chunk(kind, shard, half),
+            dst_ref=chunk(kind, shard, half),
+            send_sem=sem,
+            recv_sem=recv.at[kind, shard, half],
+            device_id=target,
+            device_id_type=MESH,
+        )
+
+    def to_sibling(kind, shard, half):
+        return remote(kind, shard, half, sib_send.at[kind, shard // 2, half], sibling)
+
+    def to_x(kind, shard):
+        return remote(kind, shard, x, x_send.at[kind, shard // 2], x_peer)
+
+    def to_y(kind, shard, half):
+        return remote(kind, shard, half, y_send.at[kind, shard // 4, half], y_peer)
+
+    def to_z(kind, step):
+        return remote(
+            kind, me, x, z_send.at[kind, step], (group, shard_of(along(step), y, core))
+        )
+
+    def arrived(kind, shard, half):
+        remote(kind, shard, half, local.at[4], sibling).wait_recv()
+
+    def begin(kind):
+        for step in range(1, depth):
+            to_z(kind, step).start()
+        to_y(kind, me, x).start()
+        to_y(kind, me, 1 - x).start()
+        for half in range(2):
+            to_sibling(kind, me, half).start()
+
+    def from_z(kind, step):
+        shard = shard_of(along(depth - step), y, core)
+        arrived(kind, shard, x)
+        to_y(kind, shard, x).start()
+        to_x(kind, shard).start()
+        to_sibling(kind, shard, x).start()
+
+    def from_own_y(kind):
+        shard = shard_of(z, 1 - y, core)
+        arrived(kind, shard, x)
+        to_sibling(kind, shard, x).start()
+        arrived(kind, shard, 1 - x)
+        to_sibling(kind, shard, 1 - x).start()
+
+    def from_y(kind, step):
+        shard = shard_of(along(depth - step), 1 - y, core)
+        arrived(kind, shard, x)
+        to_x(kind, shard).start()
+        to_sibling(kind, shard, x).start()
+
+    def from_x(kind, step, row):
+        shard = shard_of(along(depth - step), row, core)
+        arrived(kind, shard, 1 - x)
+        to_sibling(kind, shard, 1 - x).start()
+
+    copies[2].wait()
+    to_right = pltpu.make_async_remote_copy(
+        src_ref=nearby.at[:, pl.ds(patches, window), :],
+        dst_ref=nearby.at[:, pl.ds(0, window), :],
+        send_sem=halo_send.at[0],
+        recv_sem=halo_recv.at[0],
+        device_id=(group, right),
+        device_id_type=MESH,
+    )
+    to_left = pltpu.make_async_remote_copy(
+        src_ref=nearby.at[:, pl.ds(window, window), :],
+        dst_ref=nearby.at[:, pl.ds(patches + window, window), :],
+        send_sem=halo_send.at[1],
+        recv_sem=halo_recv.at[1],
+        device_id=(group, left),
+        device_id_type=MESH,
+    )
+    to_right.start()
+    to_left.start()
+    copies[0].wait()
+    begin(0)
+    copies[1].wait()
+    begin(1)
+
+    copies[3].wait()
+    block = 32
+
+    def norm_text(i, carry):
+        at = pl.ds(pl.multiple_of(i * block, block), block)
+        values = text_rows[at, :].astype(jnp.float32)
+        square = jnp.mean(values * values, axis=1, keepdims=True)
+        rows[at, :] = (values * lax.rsqrt(square + norm_epsilon) * gain_ref[...]).astype(
+            jnp.bfloat16
+        )
+        return carry
+
+    lax.fori_loop(0, text_count // block, norm_text, 0)
+    attended[...] = jnp.zeros_like(attended)
+    to_right.wait_recv()
+    to_left.wait_recv()
+
+    head_size = vis_width // VIS_HEADS
+    score_scale = 1.0 / math.sqrt(head_size)
+    span = 256
+
+    def one_head(h, carry):
+        first = h * head_size
+        start = pl.multiple_of(jnp.minimum((first // 128) * 128, vis_width - span), 128)
+        column = start + lax.broadcasted_iota(jnp.int32, (1, span), 1)
+        mine = (column >= first) & (column < first + head_size)
+        query = query_ref[:, pl.ds(start, span)].astype(jnp.float32)
+        query = jnp.where(mine, query, 0.0).astype(jnp.bfloat16)
+        scores = lax.dot_general(
+            query,
+            nearby[0, :, pl.ds(start, span)],
+            (((1,), (1,)), ((), ())),
+            preferred_element_type=jnp.float32,
+        )
+        scores = jnp.where(
+            query_id_ref[...] == key_id_ref[...], scores * score_scale, -1e30
+        )
+        shifted = jnp.exp(scores - jnp.max(scores, axis=1, keepdims=True))
+        weights = (shifted / jnp.sum(shifted, axis=1, keepdims=True)).astype(jnp.bfloat16)
+        mixed = jnp.dot(
+            weights, nearby[1, :, pl.ds(start, span)], preferred_element_type=jnp.float32
+        )
+        before = attended[:, pl.ds(start, span)].astype(jnp.float32)
+        attended[:, pl.ds(start, span)] = jnp.where(mine, mixed, before).astype(
+            jnp.bfloat16
+        )
+        return carry
+
+    third = VIS_HEADS // 4
+    lax.fori_loop(0, third, one_head, 0)
+    for step in range(1, depth):
+        from_z(0, step)
+    lax.fori_loop(third, 2 * third, one_head, 0)
+    from_own_y(0)
+    for step in range(1, depth):
+        from_y(0, step)
+        from_x(0, step, y)
+    lax.fori_loop(2 * third, 3 * third, one_head, 0)
+    for step in range(1, depth):
+        from_x(0, step, 1 - y)
+    from_z(1, 1)
+    lax.fori_loop(3 * third, 4 * third, one_head, 0)
+    for level in range(depth):
+        for row in range(2):
+            for half in range(2):
+                arrived(0, shard_of(level, row, 1 - core), half)
+
+    hidden = out_bias_ref[...] + residual_ref[...].astype(jnp.float32)
+    head_rows = out_weight.shape[1]
+    weight = out_weight[...].reshape(count * head_rows, vis_width)
+    hidden = jnp.dot(attended[...], weight, preferred_element_type=jnp.float32) + hidden
+    hidden = hidden.astype(jnp.bfloat16)
+    for part in range(2):
+        outgoing[:, :, pl.ds(part * vis_width, vis_width)] = (
+            jnp.dot(place_ref[part], hidden, preferred_element_type=jnp.float32)
+            .astype(jnp.bfloat16)
+            .reshape(count, 16, vis_width)
+        )
+
+    def row_copy(target, source):
+        return pltpu.make_async_remote_copy(
+            src_ref=outgoing.at[target],
+            dst_ref=incoming.at[me],
+            send_sem=row_send.at[target],
+            recv_sem=row_recv.at[source],
+            device_id=(group, target),
+            device_id_type=MESH,
+        )
+
+    for step in range(1, count):
+        row_copy(lax.rem(me + step, count), me).start()
+    keep = pltpu.make_async_copy(outgoing.at[me], incoming.at[me], local.at[5])
+    keep.start()
+
+    from_own_y(1)
+    for step in range(1, depth):
+        if step > 1:
+            from_z(1, step)
+        from_y(1, step)
+        from_x(1, step, y)
+
+    keep.wait()
+    for step in range(1, count):
+        source = lax.rem(me + step, count)
+        pltpu.make_async_remote_copy(
+            src_ref=outgoing.at[source],
+            dst_ref=incoming.at[source],
+            send_sem=row_send.at[source],
+            recv_sem=row_recv.at[source],
+            device_id=(group, source),
+            device_id_type=MESH,
+        ).wait_recv()
+    pair = 4
+    for i in range(count // pair):
+        values = incoming[pl.ds(i * pair, pair)].astype(jnp.float32)
+        low = values[:, :8, :].reshape(pair * 8, width // 2)
+        high = values[:, 8:, :].reshape(pair * 8, width // 2)
+        square = (
+            jnp.sum(low * low, axis=1, keepdims=True)
+            + jnp.sum(high * high, axis=1, keepdims=True)
+        ) / width
+        scale = lax.rsqrt(square + norm_epsilon)
+        at = pl.ds(text_count + i * pair * 8, pair * 8)
+        gain = gain_ref[...]
+        rows[at, : width // 2] = (low * scale * gain[:, : width // 2]).astype(jnp.bfloat16)
+        rows[at, width // 2 :] = (high * scale * gain[:, width // 2 :]).astype(jnp.bfloat16)
+
+    pieces = 4
+    piece = width // pieces
+
+    def project(number):
+        total[...] = jnp.zeros_like(total)
+
+        def add(k, carry):
+            at = pl.ds(pl.multiple_of(k * piece, 128), piece)
+            weight = jnp.concatenate(
+                [kv_weight[2 * number, at, :], kv_weight[2 * number + 1, at, :]], axis=1
+            )
+            total[...] += jnp.dot(rows[:, at], weight, preferred_element_type=jnp.float32)
+            return carry
+
+        lax.fori_loop(0, pieces, add, 0)
+        at = pl.ds(pl.multiple_of(number * 2 * LM_HEAD, 2 * LM_HEAD), 2 * LM_HEAD)
+        is_key = number * 2 < KV_HEADS
+        cosine = jnp.where(is_key, cosine_ref[...], 1.0)
+        sine = jnp.where(is_key, sine_ref[...], 0.0)
+        for side in range(2):
+            lanes = pl.ds(side * LM_HEAD, LM_HEAD)
+            here = pl.ds(
+                pl.multiple_of(number * 2 * LM_HEAD + side * LM_HEAD, LM_HEAD), LM_HEAD
+            )
+            values = total[:, lanes] + bias_ref[:, here]
+            turned = values * cosine + pltpu.roll(values, LM_HEAD // 2, 1) * sine
+            text_cache_ref[:, here] = turned[:text_count].astype(jnp.bfloat16)
+            image_cache_ref[:, here] = turned[text_count:].astype(jnp.bfloat16)
+
+    def sib_arrived(number):
+        for half in range(2):
+            arrived(1, 2 * number + 1 - core, half)
+
+    for row in range(2):
+        number = 2 * z + lax.rem(y + row, 2)
+        sib_arrived(number)
+        project(number)
+
+    def late(step, carry):
+        for row in range(2):
+            if row == 1:
+                shard = shard_of(along(depth - step), 1 - y, core)
+                arrived(1, shard, 1 - x)
+                to_sibling(1, shard, 1 - x).start()
+            number = 2 * along(depth - step) + lax.rem(y + row, 2)
+            sib_arrived(number)
+            project(number)
+        return carry
+
+    lax.fori_loop(1, depth, late, 0)
+
+    to_right.wait_send()
+    to_left.wait_send()
+    for step in range(1, count):
+        row_copy(lax.rem(me + step, count), me).wait_send()
+    for kind in range(2):
+        for level in range(depth):
+            for row in range(2):
+                for half in range(2):
+                    to_sibling(kind, shard_of(level, row, core), half).wait_send()
+        to_y(kind, me, x).wait_send()
+        to_y(kind, me, 1 - x).wait_send()
+        for step in range(1, depth):
+            to_z(kind, step).wait_send()
+            near = shard_of(along(step), y, core)
+            to_y(kind, near, x).wait_send()
+            to_x(kind, near).wait_send()
+            to_x(kind, shard_of(along(step), 1 - y, core)).wait_send()
+
+
+def turns(positions):
+    half_size = LM_HEAD // 2
+    index_pair = jnp.arange(half_size, dtype=jnp.int32)
+    frequency = jnp.power(jnp.float32(rope_base), -2.0 * index_pair.astype(jnp.float32) / LM_HEAD)
+    section = (index_pair >= half_size // 4).astype(jnp.int32) + (
+        index_pair >= half_size // 4 + 3 * half_size // 8
+    ).astype(jnp.int32)
+    places = positions.astype(jnp.float32)
+    chosen = jnp.where(
+        section[None, :] == 0,
+        places[0][:, None],
+        jnp.where(section[None, :] == 1, places[1][:, None], places[2][:, None]),
+    )
+    angles = chosen * frequency[None, :]
+    cosine, sine_part = jnp.cos(angles), jnp.sin(angles)
+    return (
+        jnp.concatenate([cosine, cosine], axis=1),
+        jnp.concatenate([-sine_part, sine_part], axis=1),
+    )
+
+
+def fused(
+    vis_query,
+    vis_keyvalue,
+    vis_residual,
+    vis_out_weight,
+    vis_out_bias,
+    image_units,
+    text_embed,
+    lm_gain,
+    lm_kv_weight,
+    lm_kv_bias,
+    text_positions,
+    image_destination,
+    image_positions,
+):
+    count = lax.axis_size("tok")
+    me = lax.axis_index("tok")
+    patches, vis_width = vis_query.shape
+    text_count, width = text_embed.shape
+    slots = image_positions.shape[1]
+    kv_width = lm_kv_bias.shape[0]
+    bounds = jnp.concatenate([jnp.zeros((1,), jnp.int32), running_sums(4 * image_units)])
+    offset = me * patches
+    query_ids = segment_ids(offset + jnp.arange(patches, dtype=jnp.int32), bounds)
+    key_ids = segment_ids(
+        offset - patches // 2 + jnp.arange(2 * patches, dtype=jnp.int32), bounds
+    )
+    target = image_destination[:, 0]
+    unit = jnp.arange(target.shape[0], dtype=jnp.int32)
+    rank = jnp.sum(
+        ((target[:, None] == target[None, :]) & (unit[None, :] < unit[:, None])).astype(jnp.int32),
+        axis=1,
+    )
+    patch = jnp.arange(patches, dtype=jnp.int32)
+    line = jnp.repeat(target * 16 + rank, 4) + 8 * (lax.rem(patch, 4) // 2)
+    lines = jnp.arange(count * 16, dtype=jnp.int32)
+    place = jnp.stack(
+        [
+            (lines[:, None] == line[None, :]) & (lax.rem(patch, 2) == part)[None, :]
+            for part in range(2)
+        ]
+    ).astype(jnp.bfloat16)
+    positions = jnp.concatenate(
+        [jnp.broadcast_to(text_positions[None, :], (3, text_count)), image_positions], axis=1
+    )
+    cosine, sine_part = turns(positions)
+    depth = count // 4
+    vmem = pl.BlockSpec(memory_space=pltpu.VMEM)
+    hbm = pl.BlockSpec(memory_space=pl.ANY)
+    bf16, f32 = jnp.bfloat16, jnp.float32
+    dma = pltpu.SemaphoreType.DMA
+    return pl.pallas_call(
+        functools.partial(fused_kernel, (count, depth)),
+        out_shape=(
+            jax.ShapeDtypeStruct((text_count, kv_width), bf16),
+            jax.ShapeDtypeStruct((slots, kv_width), bf16),
+        ),
+        in_specs=[vmem, hbm] + [vmem] * 9 + [hbm] * 3,
+        out_specs=(vmem, vmem),
+        scratch_shapes=[
+            pltpu.VMEM((count,) + vis_out_weight.shape, bf16),
+            pltpu.VMEM((count,) + lm_kv_weight.shape, bf16),
+            pltpu.VMEM((2, 2 * patches, vis_width), bf16),
+            pltpu.VMEM((patches, vis_width), bf16),
+            pltpu.VMEM((text_count, width), bf16),
+            pltpu.VMEM((text_count + slots, width), bf16),
+            pltpu.VMEM((count, 16, width // 2), bf16),
+            pltpu.VMEM((count, 16, width // 2), bf16),
+            pltpu.VMEM((text_count + slots, 2 * LM_HEAD), f32),
+            dma((2, count // 2, 2)),
+            dma((2, count // 2)),
+            dma((2, count // 4, 2)),
+            dma((2, depth)),
+            dma((2, count, 2)),
+            dma((2,)),
+            dma((2,)),
+            dma((count,)),
+            dma((count,)),
+            dma((6,)),
+        ],
+        compiler_params=pltpu.CompilerParams(
+            collective_id=0, has_side_effects=True, vmem_limit_bytes=58 * 2**20
+        ),
+    )(
+        vis_query,
+        vis_keyvalue,
+        vis_residual,
+        vis_out_bias[None, :],
+        query_ids[:, None],
+        key_ids[None, :],
+        place,
+        lm_gain[None, :],
+        lm_kv_bias[None, :],
+        cosine,
+        sine_part,
+        text_embed,
+        vis_out_weight,
+        lm_kv_weight,
+    )
+
+
+def choose(*arrays):
+    count = lax.axis_size("tok")
+    whole_tiles = (
+        lax.axis_size("groups") == 2
+        and count % 4 == 0
+        and arrays[0].shape[0] == 4 * arrays[11].shape[0]
+        and arrays[3].shape[0] % 16 == 0
+        and arrays[8].shape[1] == LM_HEAD
+        and arrays[12].shape[1] == 8 * count
+    )
+    return fused(*arrays) if whole_tiles else per_device(*arrays)
 
 
 def solution(mesh):
@@ -182,7 +701,7 @@
         P(None, ("groups", "tok")),
     )
     return jax.shard_map(
-        per_device,
+        choose,
         mesh=mesh,
         in_specs=placed,
         out_specs=(P(("groups", "tok"), None), P(("groups", "tok"), None)),

time: 233 us -> 184 us (0.79)
  Pallas kernels: 0 us -> 170 us
  waiting for transfers between devices: 136 us -> 0 us
  matrix products: 49.6 us -> 0 us
  between operations: 14.4 us -> 0.72 us
  starting transfers between devices: 10.5 us -> 0 us
  other arithmetic: 11.2 us -> 6.75 us
  local copies, waits for them, and re-layouts: 10.1 us -> 6.15 us
    pallas_call x0 -> x1, Pallas kernels: none -> 170 us  [fused(): pl.pallas_call(functools.partial(fused_kernel, (count, depth)), out_shape...]
    all_gather x2 -> x0, waiting for transfers between devices: 101 us -> none  [the longest x1 101 us: project_rows(): lax.all_gather(kv_weight, 'tok', axis=1, tiled=True)]
    dot_general x34 -> x0, matrix products: 49.6 us -> none  [the longest x16 17.9 us: head_attention(): jnp.einsum('qd,kd->qk', query_head, key_head, preferred_element_type=jnp....]
    all_to_all x1 -> x0, waiting for transfers between devices: 19.7 us -> none  [per_device(): lax.all_to_all(outgoing, 'tok', split_axis=0, concat_axis=0, tiled=True)]
    ppermute x2 -> x0, waiting for transfers between devices: 13.9 us -> none  [the longest x1 11.6 us: with_halo(): lax.ppermute(lax.slice_in_dim(block, block.shape[dim] - width, None, axis...]
    ppermute x2 -> x0, starting transfers between devices: 5.62 us -> none  [the longest x1 3.7 us: with_halo(): lax.ppermute(lax.slice_in_dim(block, block.shape[dim] - width, None, axis...]
    all_to_all x1 -> x0, starting transfers between devices: 4.8 us -> none  [per_device(): lax.all_to_all(outgoing, 'tok', split_axis=0, concat_axis=0, tiled=True)]
    reduce_sum x18 -> x2, other arithmetic: 4.56 us -> 1.02 us  [the longest x1 0.91 us: fused(): jnp.sum(((target[:, None] == target[None, :]) & (unit[None, :] < unit[:,...]
  transfers between devices with their start and end apart: 5 -> 0, of which waited for: 4 -> 0; matrix products, arithmetic and copies ran while one was open for 23% -> 0% of each run, Pallas kernels for 0% -> 0%
where the time goes in v1:
time: 184 us
  Pallas kernels  170 us (92%)
  other arithmetic  6.75 us (4%)
  local copies, waits for them, and re-layouts  6.15 us (3%)
    pallas_call x1, Pallas kernels, fused(): pl.pallas_call(functools.partial(fused_kernel, (count, depth)), out_shape...  170 us

profile of v1, /device:TPU:9, one launch (start us, length us, event | category | flops | bytes accessed | tf_op | source)
XLA Modules:
  0.0 183.7 jit_solution(4381779715898053051)
XLA Ops:
  0.6 0.7 broadcast_multiply_fusion
  1.3 0.1 select_reduce_fusion
  1.4 0.1 pad_add_fusion
  1.5 0.9 convert_reduce_fusion.2
  2.4 0.7 multiply_add_fusion.1
  3.1 0.1 convert_reduce_fusion.1
  3.2 0.1 convert_reduce_fusion
  3.3 0.6 broadcast_add_fusion
  3.9 0.7 pad.4.clone
  4.6 0.7 add_convert_fusion.1
  5.3 1.3 broadcast_in_dim.96.out_bias_ref
  6.6 0.1 broadcast_in_dim.99
  6.7 0.1 reshape.196
  6.8 0.1 fusion.1
  6.9 0.8 copy.16.query_id_ref
  7.7 0.7 add_convert_fusion.place_ref
  8.4 1.1 fusion.5
  9.5 0.9 pad_maximum_fusion
  10.4 170.0 %shard_map.140 = (bf16[256,2048]{1,0:T(8,128)(2,1)}, bf16[128,2048]{1,0:T(8,128)(2,1)}) custom-call(bf16[256,1280]{1,0:T(8,128)(2,1)} %query_ref.1, bf16[2,256,1280]{2,1,0:T(8,128)(2,1)} %keyvalue_ref.1, bf16[256,1280]{1,0:T(8,128)(2,1)} %residual_ref.1, f32[1,1280]{1,0:T(1,128)} %broadcast_in_dim.96.out_bias_ref, s32[256,1]{1,0:T(8,128)} %copy.16.query_id_ref, ...), custom_call_target="tpu_custom_call" | custom-call | tf_op jit(solution)/shard_map/pallas_call | solution.py:624
  180.5 0.0 copy-start
  180.5 2.4 %copy.19 = bf16[256,2048]{1,0:T(8,128)(2,1)} copy(bf16[256,2048]{1,0:T(8,128)(2,1)} %get-tuple-element.16) | data formatting | bytes 2097152
  182.9 0.0 copy-done
  182.9 0.8 copy.20
  (9 shorter events, 0.1 us)
Async XLA Ops:
  180.5 2.4 %copy-start = (bf16[128,2048]{1,0:T(8,128)(2,1)S(1)}, bf16[128,2048]{1,0:T(8,128)(2,1)}, u32[]{:S(2)}) copy-start(bf16[128,2048]{1,0:T(8,128)(2,1)} %get-tuple-element.17) | copy-start | bytes 1572868

commit v2 on v1

--- a/solution.py
+++ b/solution.py
@@ -214,7 +214,8 @@
     row_recv,
     local,
 ):
-    count, depth = dims
+    count, depth, ranges = dims
+    kinds = ranges + 1
     group = lax.axis_index("groups")
     me = lax.axis_index("tok")
     core = lax.rem(me, 2)
@@ -260,13 +261,15 @@
     pl.semaphore_signal(barrier, inc=1, device_id=x_peer, device_id_type=MESH)
     pl.semaphore_wait(barrier, count)
 
-    halves = (out_weight.shape[2] // 2, kv_weight.shape[1] // 2)
+    part_rows = kv_weight.shape[1] // ranges
+    halves = (out_weight.shape[2] // 2, part_rows // 2)
 
     def chunk(kind, shard, half):
-        size = halves[kind]
+        size = halves[min(kind, 1)]
         if kind == 0:
             return out_weight.at[shard, :, pl.ds(pl.multiple_of(half * size, 128), size)]
-        return kv_weight.at[shard, pl.ds(pl.multiple_of(half * size, 16), size), :]
+        first = pl.multiple_of((kind - 1) * part_rows + half * size, 16)
+        return kv_weight.at[shard, pl.ds(first, size), :]
 
     def remote(kind, shard, half, sem, target):
         return pltpu.make_async_remote_copy(
@@ -295,13 +298,18 @@
     def arrived(kind, shard, half):
         remote(kind, shard, half, local.at[4], sibling).wait_recv()
 
-    def begin(kind):
+    def begin_z(kind):
         for step in range(1, depth):
             to_z(kind, step).start()
+
+    def begin_y(kind):
         to_y(kind, me, x).start()
         to_y(kind, me, 1 - x).start()
         for half in range(2):
             to_sibling(kind, me, half).start()
+
+    def over_y(kind, step):
+        return kind % 2 == 1 and step == 1
 
     def from_z(kind, step):
         shard = shard_of(along(depth - step), y, core)
@@ -320,13 +328,34 @@
     def from_y(kind, step):
         shard = shard_of(along(depth - step), 1 - y, core)
         arrived(kind, shard, x)
-        to_x(kind, shard).start()
+        if not over_y(kind, step):
+            to_x(kind, shard).start()
         to_sibling(kind, shard, x).start()
 
-    def from_x(kind, step, row):
-        shard = shard_of(along(depth - step), row, core)
+    def from_near_x(kind, step):
+        shard = shard_of(along(depth - step), y, core)
+        arrived(kind, shard, 1 - x)
+        if over_y(kind, step):
+            to_y(kind, shard, 1 - x).start()
+        to_sibling(kind, shard, 1 - x).start()
+
+    def from_far(kind, step):
+        shard = shard_of(along(depth - step), 1 - y, core)
         arrived(kind, shard, 1 - x)
         to_sibling(kind, shard, 1 - x).start()
+
+    def tick(now):
+        if now < kinds:
+            for step in range(1, depth):
+                from_z(now, step)
+        if 0 <= now - 1 < kinds:
+            from_own_y(now - 1)
+            for step in range(1, depth):
+                from_y(now - 1, step)
+                from_near_x(now - 1, step)
+        if 0 <= now - 2 < kinds:
+            for step in range(1, depth):
+                from_far(now - 2, step)
 
     copies[2].wait()
     to_right = pltpu.make_async_remote_copy(
@@ -348,9 +377,11 @@
     to_right.start()
     to_left.start()
     copies[0].wait()
-    begin(0)
+    begin_z(0)
+    begin_y(0)
     copies[1].wait()
-    begin(1)
+    for kind in range(1, kinds):
+        begin_z(kind)
 
     copies[3].wait()
     block = 32
@@ -400,20 +431,16 @@
         )
         return carry
 
-    third = VIS_HEADS // 4
-    lax.fori_loop(0, third, one_head, 0)
-    for step in range(1, depth):
-        from_z(0, step)
-    lax.fori_loop(third, 2 * third, one_head, 0)
-    from_own_y(0)
-    for step in range(1, depth):
-        from_y(0, step)
-        from_x(0, step, y)
-    lax.fori_loop(2 * third, 3 * third, one_head, 0)
-    for step in range(1, depth):
-        from_x(0, step, 1 - y)
-    from_z(1, 1)
-    lax.fori_loop(3 * third, 4 * third, one_head, 0)
+    fourth = VIS_HEADS // 4
+    lax.fori_loop(0, fourth, one_head, 0)
+    tick(0)
+    for kind in range(1, kinds):
+        begin_y(kind)
+    lax.fori_loop(fourth, 2 * fourth, one_head, 0)
+    tick(1)
+    lax.fori_loop(2 * fourth, 3 * fourth, one_head, 0)
+    tick(2)
+    lax.fori_loop(3 * fourth, 4 * fourth, one_head, 0)
     for level in range(depth):
         for row in range(2):
             for half in range(2):
@@ -446,13 +473,7 @@
     keep = pltpu.make_async_copy(outgoing.at[me], incoming.at[me], local.at[5])
     keep.start()
 
-    from_own_y(1)
-    for step in range(1, depth):
-        if step > 1:
-            from_z(1, step)
-        from_y(1, step)
-        from_x(1, step, y)
-
+    tick(3)
     keep.wait()
     for step in range(1, count):
         source = lax.rem(me + step, count)
@@ -479,62 +500,49 @@
         rows[at, : width // 2] = (low * scale * gain[:, : width // 2]).astype(jnp.bfloat16)
         rows[at, width // 2 :] = (high * scale * gain[:, width // 2 :]).astype(jnp.bfloat16)
 
-    pieces = 4
-    piece = width // pieces
-
-    def project(number):
-        total[...] = jnp.zeros_like(total)
-
-        def add(k, carry):
-            at = pl.ds(pl.multiple_of(k * piece, 128), piece)
+    def multiply(kind):
+        depth_at = pl.ds((kind - 1) * part_rows, part_rows)
+        for level in range(depth):
+            for row in range(2):
+                for half in range(2):
+                    arrived(kind, shard_of(level, row, 1 - core), half)
+
+        def one_pair(number, carry):
             weight = jnp.concatenate(
-                [kv_weight[2 * number, at, :], kv_weight[2 * number + 1, at, :]], axis=1
+                [kv_weight[2 * number, depth_at, :], kv_weight[2 * number + 1, depth_at, :]],
+                axis=1,
             )
-            total[...] += jnp.dot(rows[:, at], weight, preferred_element_type=jnp.float32)
+            product = jnp.dot(rows[:, depth_at], weight, preferred_element_type=jnp.float32)
+            if kind > 1:
+                product = total[number] + product
+            if kind < kinds - 1:
+                total[number] = product
+                return carry
+            is_key = number * 2 < KV_HEADS
+            cosine = jnp.where(is_key, cosine_ref[...], 1.0)
+            sine = jnp.where(is_key, sine_ref[...], 0.0)
+            for side in range(2):
+                here = pl.ds(pl.multiple_of((number * 2 + side) * LM_HEAD, LM_HEAD), LM_HEAD)
+                values = product[:, side * LM_HEAD : (side + 1) * LM_HEAD] + bias_ref[:, here]
+                turned = values * cosine + pltpu.roll(values, LM_HEAD // 2, 1) * sine
+                text_cache_ref[:, here] = turned[:text_count].astype(jnp.bfloat16)
+                image_cache_ref[:, here] = turned[text_count:].astype(jnp.bfloat16)
             return carry
 
-        lax.fori_loop(0, pieces, add, 0)
-        at = pl.ds(pl.multiple_of(number * 2 * LM_HEAD, 2 * LM_HEAD), 2 * LM_HEAD)
-        is_key = number * 2 < KV_HEADS
-        cosine = jnp.where(is_key, cosine_ref[...], 1.0)
-        sine = jnp.where(is_key, sine_ref[...], 0.0)
-        for side in range(2):
-            lanes = pl.ds(side * LM_HEAD, LM_HEAD)
-            here = pl.ds(
-                pl.multiple_of(number * 2 * LM_HEAD + side * LM_HEAD, LM_HEAD), LM_HEAD
-            )
-            values = total[:, lanes] + bias_ref[:, here]
-            turned = values * cosine + pltpu.roll(values, LM_HEAD // 2, 1) * sine
-            text_cache_ref[:, here] = turned[:text_count].astype(jnp.bfloat16)
-            image_cache_ref[:, here] = turned[text_count:].astype(jnp.bfloat16)
-
-    def sib_arrived(number):
-        for half in range(2):
-            arrived(1, 2 * number + 1 - core, half)
-
-    for row in range(2):
-        number = 2 * z + lax.rem(y + row, 2)
-        sib_arrived(number)
-        project(number)
-
-    def late(step, carry):
-        for row in range(2):
-            if row == 1:
-                shard = shard_of(along(depth - step), 1 - y, core)
-                arrived(1, shard, 1 - x)
-                to_sibling(1, shard, 1 - x).start()
-            number = 2 * along(depth - step) + lax.rem(y + row, 2)
-            sib_arrived(number)
-            project(number)
-        return carry
-
-    lax.fori_loop(1, depth, late, 0)
+        lax.fori_loop(0, count // 2, one_pair, 0)
+
+    for now in range(4, kinds + 2):
+        tick(now)
+        if now - 3 >= 1:
+            multiply(now - 3)
+    for kind in range(max(1, kinds - 1), kinds):
+        multiply(kind)
 
     to_right.wait_send()
     to_left.wait_send()
     for step in range(1, count):
         row_copy(lax.rem(me + step, count), me).wait_send()
-    for kind in range(2):
+    for kind in range(kinds):
         for level in range(depth):
             for row in range(2):
                 for half in range(2):
@@ -546,7 +554,11 @@
             near = shard_of(along(step), y, core)
             to_y(kind, near, x).wait_send()
             to_x(kind, near).wait_send()
-            to_x(kind, shard_of(along(step), 1 - y, core)).wait_send()
+            back = depth - step
+            if over_y(kind, step):
+                to_y(kind, shard_of(along(back), y, core), 1 - x).wait_send()
+            else:
+                to_x(kind, shard_of(along(back), 1 - y, core)).wait_send()
 
 
 def turns(positions):
@@ -617,12 +629,13 @@
     )
     cosine, sine_part = turns(positions)
     depth = count // 4
+    ranges = 2
     vmem = pl.BlockSpec(memory_space=pltpu.VMEM)
     hbm = pl.BlockSpec(memory_space=pl.ANY)
     bf16, f32 = jnp.bfloat16, jnp.float32
     dma = pltpu.SemaphoreType.DMA
     return pl.pallas_call(
-        functools.partial(fused_kernel, (count, depth)),
+        functools.partial(fused_kernel, (count, depth, ranges)),
         out_shape=(
             jax.ShapeDtypeStruct((text_count, kv_width), bf16),
             jax.ShapeDtypeStruct((slots, kv_width), bf16),
@@ -638,12 +651,12 @@
             pltpu.VMEM((text_count + slots, width), bf16),
             pltpu.VMEM((count, 16, width // 2), bf16),
             pltpu.VMEM((count, 16, width // 2), bf16),
-            pltpu.VMEM((text_count + slots, 2 * LM_HEAD), f32),
-            dma((2, count // 2, 2)),
-            dma((2, count // 2)),
-            dma((2, count // 4, 2)),
-            dma((2, depth)),
-            dma((2, count, 2)),
+            pltpu.VMEM((count // 2, text_count + slots, 2 * LM_HEAD), f32),
+            dma((ranges + 1, count // 2, 2)),
+            dma((ranges + 1, count // 2)),
+            dma((ranges + 1, count // 4, 2)),
+            dma((ranges + 1, depth)),
+            dma((ranges + 1, count, 2)),
             dma((2,)),
             dma((2,)),
             dma((count,)),

time: 184 us -> 172 us (0.935)
  the two profiles are of different devices: /device:TPU:9 before, /device:TPU:24 now
where the time goes in v2:
time: 172 us
  Pallas kernels  158 us (92%)
  other arithmetic  6.75 us (4%)
  local copies, waits for them, and re-layouts  6.15 us (4%)
    pallas_call x1, Pallas kernels, fused(): pl.pallas_call(functools.partial(fused_kernel, (count, depth, ranges)), o...  158 us

profile of v2, /device:TPU:24, one launch (start us, length us, event | category | flops | bytes accessed | tf_op | source)
XLA Modules:
  0.0 171.9 jit_solution(17434180765997364679)
XLA Ops:
  0.6 0.7 broadcast_multiply_fusion
  1.3 0.1 select_reduce_fusion
  1.4 0.1 pad_add_fusion
  1.5 0.9 convert_reduce_fusion.2
  2.4 0.7 multiply_add_fusion.1
  3.1 0.1 convert_reduce_fusion.1
  3.2 0.1 convert_reduce_fusion
  3.3 0.6 broadcast_add_fusion
  3.9 0.7 pad.4.clone
  4.6 0.7 add_convert_fusion.1
  5.3 1.3 broadcast_in_dim.96.out_bias_ref
  6.6 0.1 broadcast_in_dim.99
  6.7 0.1 reshape.196
  6.8 0.1 fusion.1
  6.9 0.8 copy.16.query_id_ref
  7.7 0.7 add_convert_fusion.place_ref
  8.4 1.1 fusion.5
  9.5 0.9 pad_maximum_fusion
  10.4 158.3 %shard_map.140 = (bf16[256,2048]{1,0:T(8,128)(2,1)}, bf16[128,2048]{1,0:T(8,128)(2,1)}) custom-call(bf16[256,1280]{1,0:T(8,128)(2,1)} %query_ref.1, bf16[2,256,1280]{2,1,0:T(8,128)(2,1)} %keyvalue_ref.1, bf16[256,1280]{1,0:T(8,128)(2,1)} %residual_ref.1, f32[1,1280]{1,0:T(1,128)} %broadcast_in_dim.96.out_bias_ref, s32[256,1]{1,0:T(8,128)} %copy.16.query_id_ref, ...), custom_call_target="tpu_custom_call" | custom-call | tf_op jit(solution)/shard_map/pallas_call | solution.py:637
  168.7 0.0 copy-start
  168.8 2.4 %copy.19 = bf16[256,2048]{1,0:T(8,128)(2,1)} copy(bf16[256,2048]{1,0:T(8,128)(2,1)} %get-tuple-element.16) | data formatting | bytes 2097152
  171.1 0.0 copy-done
  171.1 0.8 copy.20
  (9 shorter events, 0.1 us)
Async XLA Ops:
  168.7 2.4 %copy-start = (bf16[128,2048]{1,0:T(8,128)(2,1)S(1)}, bf16[128,2048]{1,0:T(8,128)(2,1)}, u32[]{:S(2)}) copy-start(bf16[128,2048]{1,0:T(8,128)(2,1)} %get-tuple-element.17) | copy-start | bytes 1572868
